TPU v7x, 32 devices: a whole 2x2x4 slice. The times are simulated.
32 devices in a mesh: prow: 4 (over y, x), pcol: 8 (over z, core).
Axes of the slice: x: 2, y: 2, z: 4, core: 2. Of those that a mesh axis runs over, the one named last changes fastest.
Arguments:
- right_side: float32 [34, 8, 32768], P(None, 'pcol', 'prow'), may hold values from -6 to 6
- inverse_rows: float32 [34, 8, 512, 512], P(None, 'pcol', 'prow'), may hold values from -0.25 to 0.25
- panels: float32 [34, 8, 7, 512, 512], P(None, 'pcol', None, 'prow'), may hold values from -0.0625 to 0.0625
- pattern: int32 [34, 8, 7], P(None, 'pcol'), may hold values 0 or 1
- node_sizes: int32 [34, 8], P(None, 'pcol'), may hold values from 256 to 512
- parent: int32 [254], replicated, may hold values from 128 to 254, as said below
Outputs:
- solution: float32 [34, 8, 32768], P(None, 'pcol', 'prow')
Inputs may be any that keep to these rules, and one draw needn't show every extreme that they name: Nodes are numbered level by level from the leaves (128 of them, halving up to one root); entry g is the number of node g's parent, which lies on the next level up, and every node above the leaves has exactly two children.
All inputs are finite; a program needn't handle non-finite values. No bound on the sum of `pattern` on one device may be relied on, other than what follows from the above.
Results may differ from a plain program's by a relative error of at most 0.0001.
Values sent between devices are 32-bit elements; how exact they have to be, the bound alone decides.
A program may use at most 128 MiB of HBM per device.

v0:
```python
import jax
import jax.numpy as jnp
from jax import lax
from jax.sharding import PartitionSpec as P

LEVELS = 8
LEAVES = 128


def collect_updates(pending, level_slots, col_count):
    shaped = pending.reshape(level_slots, col_count, pending.shape[1])
    return lax.psum_scatter(shaped, "pcol", scatter_dimension=1, tiled=True)[:, 0]


def on_device(right_side, inverse_rows, panels, pattern, node_sizes, parent):
    col_count = lax.axis_size("pcol")
    col_index = lax.axis_index("pcol")
    row_index = lax.axis_index("prow")
    part_rows = panels.shape[3]
    full_rows = panels.shape[4]
    rhs_count = right_side.shape[2] // part_rows
    piece_len = part_rows * rhs_count
    node_counts = [LEAVES >> height for height in range(LEVELS)]
    slot_counts = [max(1, count_here // col_count) for count_here in node_counts]
    pending = {}
    for height in range(1, LEVELS):
        pending[height] = jnp.zeros((slot_counts[height] * col_count, piece_len), jnp.float32)
    row_ids = row_index * part_rows + jnp.arange(part_rows, dtype=jnp.int32)
    full_ids = jnp.arange(full_rows, dtype=jnp.int32)
    outputs = []
    node_base = 0
    slot_base = 0
    for height in range(LEVELS):
        level_nodes = node_counts[height]
        level_slots = slot_counts[height]
        local_nodes = jnp.arange(level_slots, dtype=jnp.int32) * col_count + col_index
        is_real = local_nodes < level_nodes
        node_ids = node_base + jnp.minimum(local_nodes, level_nodes - 1)
        residue = right_side[slot_base : slot_base + level_slots, 0]
        if height > 0:
            residue = residue - collect_updates(pending[height], level_slots, col_count)
        live_limit = node_sizes[slot_base : slot_base + level_slots, 0]
        keep_rows = ((row_ids[None, :] < live_limit[:, None]) & is_real[:, None]).astype(
            jnp.float32
        )
        keep_full = ((full_ids[None, :] < live_limit[:, None]) & is_real[:, None]).astype(
            jnp.float32
        )
        scaled = residue.reshape(level_slots, part_rows, rhs_count) * keep_rows[:, :, None]
        inverse = inverse_rows[slot_base : slot_base + level_slots, 0]
        partial_term = jnp.einsum("nvw,nvq->nwq", inverse, scaled, precision=lax.Precision.HIGHEST)
        partial_term = partial_term.reshape(level_slots, full_rows * rhs_count)
        solved = None
        summed = lax.psum(partial_term, "prow")
        solved = summed.reshape(level_slots, full_rows, rhs_count) * keep_full[:, :, None]
        own_rows = lax.dynamic_slice_in_dim(solved, row_index * part_rows, part_rows, 1)
        outputs.append(own_rows.reshape(level_slots, piece_len))
        reach = LEVELS - 1 - height
        if reach > 0:
            panel_rows = panels[slot_base : slot_base + level_slots, 0, :reach]
            contrib = jnp.einsum(
                "napw,nwq->napq", panel_rows, solved, precision=lax.Precision.HIGHEST
            )
            block_mask = pattern[slot_base : slot_base + level_slots, 0, :reach].astype(
                jnp.float32
            ) * is_real[:, None].astype(jnp.float32)
            contrib = contrib * block_mask[:, :, None, None]
            ancestor = node_ids
            target_base = node_base + level_nodes
            for distance in range(reach):
                ancestor = parent[ancestor]
                target = height + 1 + distance
                target_rows = slot_counts[target] * col_count
                onehot = (
                    (ancestor - target_base)[:, None]
                    == jnp.arange(target_rows, dtype=jnp.int32)[None, :]
                ).astype(jnp.float32)
                addition = jnp.einsum(
                    "nt,nx->tx",
                    onehot,
                    contrib[:, distance].reshape(level_slots, piece_len),
                    precision=lax.Precision.HIGHEST,
                )
                pending[target] = pending[target] + addition
                target_base = target_base + node_counts[target]
        node_base = node_base + level_nodes
        slot_base = slot_base + level_slots
    return jnp.concatenate(outputs, 0)[:, None, :]


def solution(mesh):
    in_specs = (
        P(None, "pcol", "prow"),
        P(None, "pcol", "prow", None),
        P(None, "pcol", None, "prow", None),
        P(None, "pcol", None),
        P(None, "pcol"),
        P(),
    )
    out_specs = P(None, "pcol", "prow")
    return jax.shard_map(
        on_device, mesh=mesh, in_specs=in_specs, out_specs=out_specs, check_vma=False
    )
```

profile of v0, /device:TPU:0, one launch (start us, length us, event | category | flops | bytes accessed | tf_op | source)
XLA Modules:
  0.0 910.5 jit_solution(3661712038669378163)
XLA Ops:
  6.5 2.4 slice_reduce_fusion
  10.2 6.4 fusion.21
  55.1 34.0 %all-reduce.21.cloned.1.call-done = f32[16,512,64]{1,2,0:T(8,128)} async-done(((f32[16,512,64]{1,2,0:T(8,128)}), f32[16,512,64]{1,2,0:T(8,128)}) %all-reduce.21.cloned.1.call-update) | async-done | bytes 2097168 | tf_op jit(solution)/shard_map/psum | solution.py:54
  90.9 31.5 %multiply_bitcast_fusion = f32[16,7,128,64]{2,3,1,0:T(8,128)S(1)} fusion(f32[16,7]{1,0:T(8,128)S(1)} %copy.148, f32[34,1,7,128,512]{4,3,2,0,1:T(8,128)} %bitcast.436, f32[16,512,64]{1,2,0:T(8,128)S(1)} %broadcast_multiply_fusion), kind=kOutput, calls=%fused_computation.57 | convolution fusion | flops 5638062080 | bytes 35127744 | tf_op jit(solution)/shard_map/napw,nwq->napq/dot_general | solution.py:61
  126.8 3.4 fusion.75
  151.2 15.0 %reduce-scatter.6.cloned.1.call-done = f32[8,1,8192]{2,0,1:T(8,128)} async-done(((f32[8,8,8192]{2,0,1:T(8,128)}), f32[8,1,8192]{2,0,1:T(8,128)}) %reduce-scatter.6.cloned.1.call-update) | async-done | bytes 262160 | tf_op jit(solution)/shard_map/reduce_scatter | solution.py:12
  167.6 4.0 fusion.22
  180.0 2.1 fusion.82
  184.2 2.7 fusion.79
  187.0 36.2 %all-reduce.23.cloned.1.call-done = f32[8,512,64]{1,2,0:T(8,128)} async-done(((f32[8,512,64]{1,2,0:T(8,128)}), f32[8,512,64]{1,2,0:T(8,128)}) %all-reduce.23.cloned.1.call-update) | async-done | bytes 1048592 | tf_op jit(solution)/shard_map/psum | solution.py:54
  224.5 14.8 %multiply_bitcast_fusion.1 = f32[8,6,128,64]{2,3,1,0:T(8,128)S(1)} fusion(f32[34,1,7,128,512]{4,3,2,0,1:T(8,128)} %bitcast.437, f32[8,512,64]{1,2,0:T(8,128)S(1)} %broadcast_multiply_fusion.1, f32[8,6]{1,0:T(8,128)S(1)} %bitcast_multiply_fusion), kind=kOutput, calls=%fused_computation.64 | convolution fusion | flops 2416312320 | bytes 15204544 | tf_op jit(solution)/shard_map/napw,nwq->napq/dot_general | solution.py:61
  256.6 2.2 fusion.84
  261.9 45.1 %all-reduce.37.cloned.1.call-done = f32[4,8,8192]{2,0,1:T(4,128)} async-done(((f32[4,8,8192]{2,0,1:T(4,128)}), f32[4,8,8192]{2,0,1:T(4,128)}) %all-reduce.37.cloned.1.call-update) | async-done | bytes 1048592
  308.9 2.8 convolution_bitcast_fusion
  319.7 36.5 %all-reduce.25.cloned.1.call-done = f32[4,512,64]{1,2,0:T(8,128)} async-done(((f32[4,512,64]{1,2,0:T(8,128)}), f32[4,512,64]{1,2,0:T(8,128)}) %all-reduce.25.cloned.1.call-update) | async-done | bytes 524304 | tf_op jit(solution)/shard_map/psum | solution.py:54
  357.3 7.0 fusion.24
  372.1 51.5 %all-reduce.39.cloned.1.call-done = f32[2,8,8192]{2,0,1:T(2,128)} async-done(((f32[2,8,8192]{2,0,1:T(2,128)}), f32[2,8,8192]{2,0,1:T(2,128)}) %all-reduce.39.cloned.1.call-update) | async-done | bytes 524304
  425.4 2.3 convolution_bitcast_fusion.1
  430.6 39.1 %all-reduce.27.cloned.1.call-done = f32[2,512,64]{1,2,0:T(8,128)} async-done(((f32[2,512,64]{1,2,0:T(8,128)}), f32[2,512,64]{1,2,0:T(8,128)}) %all-reduce.27.cloned.1.call-update) | async-done | bytes 262160 | tf_op jit(solution)/shard_map/psum | solution.py:54
  470.7 3.7 fusion.26
  484.1 48.8 %all-reduce.41.cloned.1.call-done = f32[1,8,8192]{2,1,0:T(8,128)} async-done(((f32[1,8,8192]{2,1,0:T(8,128)}), f32[1,8,8192]{2,1,0:T(8,128)}) %all-reduce.41.cloned.1.call-update) | async-done | bytes 262160
  539.2 39.0 %all-reduce.29.cloned.1.call-done = f32[1,32768]{1,0:T(1,128)} async-done(((f32[1,32768]{1,0:T(1,128)}), f32[1,32768]{1,0:T(1,128)}) %all-reduce.29.cloned.1.call-update) | async-done | bytes 131088 | tf_op jit(solution)/shard_map/psum | solution.py:54
  578.6 2.8 multiply_reduce_fusion.2
  581.6 2.1 fusion.27
  587.6 53.7 %all-reduce.43.cloned.1.call-done = f32[1,8,8192]{2,1,0:T(8,128)} async-done(((f32[1,8,8192]{2,1,0:T(8,128)}), f32[1,8,8192]{2,1,0:T(8,128)}) %all-reduce.43.cloned.1.call-update) | async-done | bytes 262160
  648.6 38.0 %all-reduce.31.cloned.1.call-done = f32[1,32768]{1,0:T(1,128)} async-done(((f32[1,32768]{1,0:T(1,128)}), f32[1,32768]{1,0:T(1,128)}) %all-reduce.31.cloned.1.call-update) | async-done | bytes 131088 | tf_op jit(solution)/shard_map/psum | solution.py:54
  686.7 2.8 multiply_reduce_fusion.1
  696.7 52.4 %all-reduce.45.cloned.1.call-done = f32[1,8,8192]{2,1,0:T(8,128)} async-done(((f32[1,8,8192]{2,1,0:T(8,128)}), f32[1,8,8192]{2,1,0:T(8,128)}) %all-reduce.45.cloned.1.call-update) | async-done | bytes 262160
  756.2 38.1 %all-reduce.33.cloned.1.call-done = f32[1,32768]{1,0:T(1,128)} async-done(((f32[1,32768]{1,0:T(1,128)}), f32[1,32768]{1,0:T(1,128)}) %all-reduce.33.cloned.1.call-update) | async-done | bytes 131088 | tf_op jit(solution)/shard_map/psum | solution.py:54
  794.4 2.2 multiply_reduce_fusion
  801.2 54.1 %all-reduce.47.cloned.1.call-done = f32[1,8,8192]{2,1,0:T(8,128)} async-done(((f32[1,8,8192]{2,1,0:T(8,128)}), f32[1,8,8192]{2,1,0:T(8,128)}) %all-reduce.47.cloned.1.call-update) | async-done | bytes 262160
  859.3 40.9 %all-reduce.35.cloned.1.call-done = f32[1,512,64]{1,2,0:T(8,128)} async-done(((f32[1,512,64]{1,2,0:T(8,128)}), f32[1,512,64]{1,2,0:T(8,128)}) %all-reduce.35.cloned.1.call-update) | async-done | bytes 131088 | tf_op jit(solution)/shard_map/psum | solution.py:54
  (391 shorter events, 168.1 us)
Async XLA Ops:
  6.5 82.5 %all-reduce.21.cloned.1.call-start = ((), (), s32[]{:S(2)}) async-start(), calls=%async_computation.1 | async-start | bytes 4194304 | tf_op jit(solution)/shard_map/psum | solution.py:54
  16.6 149.7 %reduce-scatter.6.cloned.1.call-start = ((), (), s32[]{:S(2)}) async-start(), calls=%async_computation.2 | async-start | bytes 2359296 | tf_op jit(solution)/shard_map/reduce_scatter | solution.py:12
  130.2 92.9 %all-reduce.23.cloned.1.call-start = ((), (), s32[]{:S(2)}) async-start(), calls=%async_computation.3 | async-start | bytes 2097152 | tf_op jit(solution)/shard_map/psum | solution.py:54
  171.7 135.3 %all-reduce.37.cloned.1.call-start = ((), (), s32[]{:S(2)}) async-start(), calls=%async_computation.10 | async-start | bytes 2097152
  248.0 108.2 %all-reduce.25.cloned.1.call-start = ((), (), s32[]{:S(2)}) async-start(), calls=%async_computation.4 | async-start | bytes 1048576 | tf_op jit(solution)/shard_map/psum | solution.py:54
  258.8 59.4 %copy-start.4 = (f32[16,8192]{1,0:T(8,128)S(1)}, f32[16,8192]{1,0:T(8,128)}, u32[]{:S(2)}) copy-start(f32[16,8192]{1,0:T(8,128)} %reshape_squeeze.79) | copy-start | bytes 1572868
  311.7 111.9 %all-reduce.39.cloned.1.call-start = ((), (), s32[]{:S(2)}) async-start(), calls=%async_computation.11 | async-start | bytes 1048576
  364.4 59.2 %slice-start.2 = ((f32[34,1,8192]{2,1,0:T(1,128)}), f32[2,1,8192]{2,1,0:T(1,128)S(1)}, s32[]{:S(2)}) async-start(f32[34,1,8192]{2,1,0:T(1,128)} %param.6), calls=%async_computation.18 | async-start | bytes 131072 | tf_op jit(solution)/shard_map/slice | solution.py:39
  364.4 61.0 %copy-start.15 = (f32[2,128]{1,0:T(2,128)S(1)}, f32[2,128]{1,0:T(2,128)}, u32[]{:S(2)}) copy-start(f32[2,128]{1,0:T(2,128)} %and_convert_fusion.7) | copy-start | bytes 3076
  366.0 62.9 %copy-start.9 = (f32[4,1,128,64]{2,3,1,0:T(8,128)S(1)}, f32[4,1,128,64]{2,3,1,0:T(8,128)}, u32[]{:S(2)}) copy-start(f32[4,1,128,64]{2,3,1,0:T(8,128)} %get-tuple-element.93) | copy-start | bytes 393220
  367.2 103.4 %copy-start.14 = (f32[2,4]{1,0:T(2,128)S(1)}, f32[2,4]{1,0:T(2,128)}, u32[]{:S(2)}) copy-start(f32[2,4]{1,0:T(2,128)} %bitcast_multiply_fusion.2) | copy-start | bytes 100
  367.3 102.4 %all-reduce.27.cloned.1.call-start = ((), (), s32[]{:S(2)}) async-start(), calls=%async_computation.5 | async-start | bytes 524288 | tf_op jit(solution)/shard_map/psum | solution.py:54
  427.6 105.2 %all-reduce.41.cloned.1.call-start = ((), (), s32[]{:S(2)}) async-start(), calls=%async_computation.12 | async-start | bytes 524288
  428.8 104.1 %copy-start.5 = (f32[34,1,8192]{2,1,0:T(1,128)S(1)}, f32[34,1,8192]{2,1,0:T(1,128)}, u32[]{:S(2)}) copy-start(f32[34,1,8192]{2,1,0:T(1,128)} %param.6) | copy-start | bytes 3342340
  429.2 107.9 %copy-start.7 = (f32[8,8192]{1,0:T(8,128)S(1)}, f32[8,8192]{1,0:T(8,128)}, u32[]{:S(2)}) copy-start(f32[8,8192]{1,0:T(8,128)} %convolution_add_fusion.11) | copy-start | bytes 786436
  470.7 110.9 %copy-start.16 = (f32[3]{0:T(128)S(1)}, f32[3]{0:T(128)}, u32[]{:S(2)}) copy-start(f32[3]{0:T(128)} %multiply_reduce_fusion.3) | copy-start | bytes 40
  474.4 110.1 %copy-start.25 = (f32[8]{0:T(128)S(1)}, f32[8]{0:T(128)}, u32[]{:S(2)}) copy-start(f32[8]{0:T(128)} %fusion.122) | copy-start | bytes 100
  477.8 165.4 %copy-start.20 = (f32[128]{0:T(128)S(1)}, f32[128]{0:T(128)}, u32[]{:S(2)}) copy-start(f32[128]{0:T(128)} %and_convert_fusion.5) | copy-start | bytes 1540
  477.9 100.3 %all-reduce.29.cloned.1.call-start = ((), (), s32[]{:S(2)}) async-start(), calls=%async_computation.6 | async-start | bytes 262144 | tf_op jit(solution)/shard_map/psum | solution.py:54
  484.1 205.5 %copy-start.17 = (f32[2]{0:T(128)S(1)}, f32[2]{0:T(128)}, u32[]{:S(2)}) copy-start(f32[2]{0:T(128)} %multiply_reduce_fusion.4) | copy-start | bytes 28
  537.0 104.3 %all-reduce.43.cloned.1.call-start = ((), (), s32[]{:S(2)}) async-start(), calls=%async_computation.13 | async-start | bytes 524288
  583.7 167.2 %copy-start.18 = (f32[128]{0:T(128)S(1)}, f32[128]{0:T(128)}, u32[]{:S(2)}) copy-start(f32[128]{0:T(128)} %and_convert_fusion.4) | copy-start | bytes 1540
  586.3 100.4 %all-reduce.31.cloned.1.call-start = ((), (), s32[]{:S(2)}) async-start(), calls=%async_computation.7 | async-start | bytes 262144 | tf_op jit(solution)/shard_map/psum | solution.py:54
  645.5 103.6 %all-reduce.45.cloned.1.call-start = ((), (), s32[]{:S(2)}) async-start(), calls=%async_computation.14 | async-start | bytes 524288
  646.8 151.5 %copy-start.21 = (f32[8]{0:T(128)S(1)}, f32[8]{0:T(128)}, u32[]{:S(2)}) copy-start(f32[8]{0:T(128)} %get-tuple-element.115) | copy-start | bytes 100
  689.6 167.5 %copy-start.19 = (f32[128]{0:T(128)S(1)}, f32[128]{0:T(128)}, u32[]{:S(2)}) copy-start(f32[128]{0:T(128)} %and_convert_fusion.3) | copy-start | bytes 1540
  691.2 64.0 %copy-start.8 = (f32[32768]{0:T(1024)S(1)}, f32[32768]{0:T(1024)}, u32[]{:S(2)}) copy-start(f32[32768]{0:T(1024)} %get-tuple-element.74) | copy-start | bytes 393220
  691.2 167.8 %copy-start.22 = (f32[128]{0:T(128)S(1)}, f32[128]{0:T(128)}, u32[]{:S(2)}) copy-start(f32[128]{0:T(128)} %dynamic-slice.32) | copy-start | bytes 1540
  692.0 209.2 %copy-start.3 = (f32[16,8192]{1,0:T(8,128)S(1)}, f32[16,8192]{1,0:T(8,128)}, u32[]{:S(2)}) copy-start(f32[16,8192]{1,0:T(8,128)} %reshape.1816) | copy-start | bytes 1572868
  694.0 100.4 %all-reduce.33.cloned.1.call-start = ((), (), s32[]{:S(2)}) async-start(), calls=%async_computation.8 | async-start | bytes 262144 | tf_op jit(solution)/shard_map/psum | solution.py:54
  753.2 102.0 %all-reduce.47.cloned.1.call-start = ((), (), s32[]{:S(2)}) async-start(), calls=%async_computation.15 | async-start | bytes 524288
  800.2 100.0 %all-reduce.35.cloned.1.call-start = ((), (), s32[]{:S(2)}) async-start(), calls=%async_computation.9 | async-start | bytes 262144 | tf_op jit(solution)/shard_map/psum | solution.py:54
  (16 other events, 475.2 us)
Sparse Core Ops, SparseCore 0:
  16.7 72.3 all-reduce.20
  130.4 35.8 reduce-scatter.5
  171.8 51.2 all-reduce.22
  248.1 58.8 all-reduce.36
  311.9 44.2 all-reduce.24
  367.4 56.1 all-reduce.38
  427.8 41.8 all-reduce.26
  478.0 54.8 all-reduce.40
  537.1 40.9 all-reduce.28
  586.4 54.9 all-reduce.42
  645.6 40.9 all-reduce.30
  694.1 54.9 all-reduce.44
  753.3 40.9 all-reduce.32
  800.3 54.9 all-reduce.46
  859.2 40.9 all-reduce.34
where the time goes:
time: 917 us; the launch traced here: 911 us
  waiting for transfers between devices  623 us (68%)
  matrix products  123 us (13%)
  local copies, waits for them, and re-layouts  87.1 us (9%)
  other arithmetic  51 us (6%)
  between operations  24.6 us (3%)
    unnamed x21, waiting for transfers between devices  306 us
    psum x8, waiting for transfers between devices, on_device(): summed = lax.psum(partial_term, 'prow')  302 us
    dot_general x7, matrix products, on_device(): jnp.einsum('napw,nwq->napq', panel_rows, solved, precision=lax.Precision....  62.4 us
    dot_general x22, matrix products, on_device(): jnp.einsum('nt,nx->tx', onehot, contrib[:, distance].reshape(level_slots,...  39.2 us
    slice x33, local copies, waits for them, and re-layouts, on_device(): contrib[:, distance].reshape(level_slots, piece_len)  28 us
    dot_general x8, matrix products, on_device(): jnp.einsum('nvw,nvq->nwq', inverse, scaled, precision=lax.Precision.HIGHEST)  21.4 us
  transfers between devices with their start and end apart: 15, of which 15 were waited for; matrix products, arithmetic and copies ran while one was open for 12% of the time, Pallas kernels for 0%

commit v1 on v0

v1 whole, which is shorter than its diff:
```python
import functools

import jax
import jax.numpy as jnp
from jax import lax
from jax.experimental import pallas as pl
from jax.experimental.pallas import tpu as pltpu
from jax.sharding import PartitionSpec as P

LEVELS = 8
LEAVES = 128
GROUP = 4
RING = 12
MESH = pl.DeviceIdType.MESH


class Plan:
    def __init__(self, rows, cols):
        self.rows, self.cols = rows, cols
        self.depth = cols // 2
        self.nodes = [LEAVES >> h for h in range(LEVELS)]
        self.slots = [max(1, n // cols) for n in self.nodes]
        self.slot_base, self.node_base, self.pend_base = [], [], []
        self.half_base, self.far_base = [], []
        s = n = p = c = f = 0
        for h in range(LEVELS):
            self.slot_base.append(s)
            self.node_base.append(n)
            self.pend_base.append(p)
            self.half_base.append(c)
            self.far_base.append(f)
            s += self.slots[h]
            n += self.nodes[h]
            if h > 0:
                p += self.slots[h] * cols
                c += self.slots[h] * self.depth
                f += self.slots[h] * (self.depth - 1)
        self.total, self.pend, self.half, self.far = s, p, c, f
        self.groups = []
        for h in range(LEVELS):
            size = min(GROUP, self.slots[h])
            for start in range(0, self.slots[h], size):
                self.groups.append((h, self.slot_base[h] + start, size))
        self.level_of = [h for h in range(LEVELS) for _ in range(self.slots[h])]


def split_pair(packed, low_lanes):
    high = packed.astype(jnp.bfloat16).astype(jnp.float32)
    low = packed - high
    top = jnp.where(low_lanes, high, pltpu.roll(low, 64, 1))
    bottom = jnp.where(low_lanes, pltpu.roll(high, 64, 1), low)
    return jnp.concatenate([top, bottom], 0).astype(jnp.bfloat16)


def two_part(matrix):
    high = matrix.astype(jnp.bfloat16)
    low = (matrix - high.astype(jnp.float32)).astype(jnp.bfloat16)
    return high, low


def kernel(
    plan, parent, pattern, sizes, rhs, inverse_hbm, panels_hbm, out,
    inverse, ring, pend, near, far, parts, arrived, solved, wide, blocks,
    target, weight, live,
    inverse_sem, ring_sem, near_sem, far_send, far_recv, part_send, part_recv, sol_send, sol_recv,
):
    rows, cols, depth = plan.rows, plan.cols, plan.depth
    piece = inverse.shape[1]
    half = piece // 2
    my_row, my_col = lax.axis_index("prow"), lax.axis_index("pcol")
    my_core, my_z = lax.rem(my_col, 2), lax.div(my_col, 2)
    row_peers = [lax.rem(my_row + d, rows) for d in range(1, rows)]
    z_peers = [lax.rem(my_z + d, depth) for d in range(1, depth)]
    mate = my_col + 1 - 2 * my_core

    loads = []
    for h in range(LEVELS):
        span = pl.ds(plan.slot_base[h], plan.slots[h])
        copy = pltpu.make_async_copy(inverse_hbm.at[span], inverse.at[span], inverse_sem.at[h])
        copy.start()
        loads.append(copy)
    panel_loads = {}

    def load_panel(slot):
        if slot >= plan.total:
            return
        reach = LEVELS - 1 - plan.level_of[slot]
        if reach == 0:
            return
        place = slot % RING
        copy = pltpu.make_async_copy(
            panels_hbm.at[slot, pl.ds(0, reach)], ring.at[place, pl.ds(0, reach)], ring_sem.at[place]
        )
        copy.start()
        panel_loads[slot] = copy

    for slot in range(min(RING, plan.total)):
        load_panel(slot)

    barrier = pltpu.get_barrier_semaphore()
    greeted = [(p, my_col) for p in row_peers] + [(my_row, mate)]
    greeted += [(my_row, z * 2 + my_core) for z in z_peers]
    for who in greeted:
        pl.semaphore_signal(barrier, inc=1, device_id=who, device_id_type=MESH)

    for h in range(LEVELS):

        def describe(i, carry, h=h):
            slot = plan.slot_base[h] + i
            place = i * cols + my_col
            real = place < plan.nodes[h]
            live[slot] = jnp.where(real, sizes[slot], 0)
            node = plan.node_base[h] + jnp.minimum(place, plan.nodes[h] - 1)
            for a in range(LEVELS - 1 - h):
                up = h + 1 + a
                node = parent[node]
                local = node - plan.node_base[up]
                owner = lax.rem(local, cols)
                spot = lax.rem(owner, 2) * depth + lax.div(owner, 2)
                target[slot * 7 + a] = spot * plan.slots[up] + lax.div(local, cols)
                weight[slot * 7 + a] = jnp.where(real, pattern[slot * 7 + a], 0).astype(jnp.float32)
            return carry

        lax.fori_loop(0, plan.slots[h], describe, 0)

    def clear(i, carry):
        pend[i] = jnp.zeros_like(pend[i])
        return carry

    lax.fori_loop(0, plan.pend, clear, 0)

    lane = lax.broadcasted_iota(jnp.int32, (half, 128), 1)
    low_lanes = lane < 64
    row_ids = (
        my_row * piece
        + lax.broadcasted_iota(jnp.int32, (half, 128), 0)
        + jnp.where(low_lanes, 0, half)
    )
    contract_first = (((0,), (0,)), ((), ()))
    sends = []

    pl.semaphore_wait(barrier, len(greeted))

    def remote(src, dst, send_sem, recv_sem, who):
        copy = pltpu.make_async_remote_copy(
            src_ref=src, dst_ref=dst, send_sem=send_sem, recv_sem=recv_sem,
            device_id=who, device_id_type=MESH,
        )
        copy.start()
        sends.append(copy)
        return copy

    def start_partial(g):
        h, base, size = plan.groups[g]

        def body(n, carry):
            slot = base + n
            residue = rhs[slot]
            if h > 0:
                step = slot - plan.slot_base[h]
                own = (my_core * depth + my_z) * plan.slots[h] + step
                update = pend[plan.pend_base[h] + own]
                for d in range(depth - 1):
                    update = update + far[plan.far_base[h] + d * plan.slots[h] + step]
                residue = residue - update
            scaled = jnp.where(row_ids < live[slot], residue, 0.0)
            pair = split_pair(scaled, low_lanes)
            high, low = two_part(inverse[slot])
            both = lax.dot_general(high, pair, contract_first, preferred_element_type=jnp.float32)
            both += lax.dot_general(low, pair, contract_first, preferred_element_type=jnp.float32)
            both += pltpu.roll(both, 64, 1)
            for r in range(rows):
                first = both[r * piece : r * piece + half]
                second = both[r * piece + half : (r + 1) * piece]
                parts[r, slot] = jnp.where(low_lanes, first, second)
            return carry

        lax.fori_loop(0, size, body, 0)
        span = pl.ds(base, size)
        return [
            remote(
                parts.at[peer, span], arrived.at[d, span],
                part_send.at[g, d], part_recv.at[g, d], (peer, my_col),
            )
            for d, peer in enumerate(row_peers)
        ]

    def start_solved(g, copies):
        h, base, size = plan.groups[g]
        for copy in copies:
            copy.wait_recv()

        def body(n, carry):
            slot = base + n
            total = parts[my_row, slot]
            for d in range(rows - 1):
                total = total + arrived[d, slot]
            total = jnp.where(row_ids < live[slot], total, 0.0)
            solved[my_row, slot] = total
            out[slot] = total
            return carry

        lax.fori_loop(0, size, body, 0)
        if h == LEVELS - 1:
            return []
        span = pl.ds(base, size)
        return [
            remote(
                solved.at[my_row, span], solved.at[my_row, span],
                sol_send.at[g, d], sol_recv.at[g, d], (peer, my_col),
            )
            for d, peer in enumerate(row_peers)
        ]

    def widen(g, copies):
        h, base, size = plan.groups[g]
        for copy in copies:
            copy.wait_recv()

        def body(n, carry):
            for r in range(rows):
                wide[n, pl.ds(r * piece, piece)] = split_pair(solved[r, base + n], low_lanes)
            return carry

        lax.fori_loop(0, size, body, 0)
        for slot in range(base, base + size):
            panel_loads[slot].wait()

    def contribute(g, first, last):
        h, base, size = plan.groups[g]
        if first >= last:
            return

        def body(n, carry):
            place = lax.rem(base + n, RING)
            pair = wide[n]
            for a in range(first, last):
                high, low = two_part(ring[place, a])
                both = jnp.dot(high, pair, preferred_element_type=jnp.float32)
                both += jnp.dot(low, pair, preferred_element_type=jnp.float32)
                both += pltpu.roll(both, 64, 1)
                blocks[n, a] = jnp.where(low_lanes, both[:half], both[half:])
            return carry

        lax.fori_loop(0, size, body, 0)
        for a in range(first, last):
            up = h + 1 + a
            goals = [target[(base + n) * 7 + a] for n in range(size)]
            scales = [weight[(base + n) * 7 + a] for n in range(size)]

            def scatter(t, carry, a=a, up=up, goals=goals, scales=scales):
                total = pend[plan.pend_base[up] + t]
                for n in range(size):
                    total = total + jnp.where(goals[n] == t, scales[n], 0.0) * blocks[n, a]
                pend[plan.pend_base[up] + t] = total
                return carry

            lax.fori_loop(0, plan.slots[up] * cols, scatter, 0)

    def start_near(h):
        count = plan.slots[h] * depth
        return remote(
            pend.at[pl.ds(plan.pend_base[h] + (1 - my_core) * count, count)],
            near.at[pl.ds(plan.half_base[h], count)],
            near_sem.at[0, h], near_sem.at[1, h], (my_row, mate),
        )

    def start_far(h, copy):
        count = plan.slots[h] * depth
        mine = plan.pend_base[h] + my_core * count
        copy.wait_recv()

        def body(i, carry):
            pend[mine + i] = pend[mine + i] + near[plan.half_base[h] + i]
            return carry

        lax.fori_loop(0, count, body, 0)
        return [
            remote(
                pend.at[pl.ds(mine + z * plan.slots[h], plan.slots[h])],
                far.at[pl.ds(plan.far_base[h] + d * plan.slots[h], plan.slots[h])],
                far_send.at[h, d], far_recv.at[h, d], (my_row, z * 2 + my_core),
            )
            for d, z in enumerate(z_peers)
        ]

    group_ids = {h: [g for g, one in enumerate(plan.groups) if one[0] == h] for h in range(LEVELS)}
    for h in range(LEVELS):
        reach = LEVELS - 1 - h
        ids = group_ids[h]
        loads[h].wait()
        waiting = [start_partial(g) for g in ids]
        sharing = {ids[0]: start_solved(ids[0], waiting[0])}
        for i, g in enumerate(ids):
            if i + 1 < len(ids):
                sharing[ids[i + 1]] = start_solved(ids[i + 1], waiting[i + 1])
            if reach == 0:
                continue
            widen(g, sharing[g])
            final = i + 1 == len(ids)
            contribute(g, 0, 1)
            if final:
                near_copy = start_near(h + 1)
            contribute(g, 1, min(2, reach))
            if final:
                far_copies = start_far(h + 1, near_copy)
            contribute(g, 2, reach)
            _, base, size = plan.groups[g]
            for slot in range(base, base + size):
                load_panel(slot + RING)
            if final:
                for copy in far_copies:
                    copy.wait_recv()
    for copy in sends:
        copy.wait_send()


def on_device(right_side, inverse_rows, panels, pattern, node_sizes, parent):
    rows, cols = lax.axis_size("prow"), lax.axis_size("pcol")
    plan = Plan(rows, cols)
    slots, piece, full = plan.total, panels.shape[3], panels.shape[4]
    count = right_side.shape[2] // piece
    half = piece // 2
    packed = right_side.reshape(slots, 2, half, count).swapaxes(1, 2).reshape(slots, half, 2 * count)
    groups = len(plan.groups)
    dma = pltpu.SemaphoreType.DMA
    vmem = pl.BlockSpec(memory_space=pltpu.VMEM)
    smem = pl.BlockSpec(memory_space=pltpu.SMEM)
    anywhere = pl.BlockSpec(memory_space=pl.ANY)
    block = (half, 2 * count)
    solved = pl.pallas_call(
        functools.partial(kernel, plan),
        out_shape=jax.ShapeDtypeStruct((slots,) + block, jnp.float32),
        in_specs=[smem, smem, smem, vmem, anywhere, anywhere],
        out_specs=vmem,
        scratch_shapes=[
            pltpu.VMEM((slots, piece, full), jnp.float32),
            pltpu.VMEM((RING, LEVELS - 1, piece, full), jnp.float32),
            pltpu.VMEM((plan.pend,) + block, jnp.float32),
            pltpu.VMEM((plan.half,) + block, jnp.float32),
            pltpu.VMEM((plan.far,) + block, jnp.float32),
            pltpu.VMEM((rows, slots) + block, jnp.float32),
            pltpu.VMEM((rows - 1, slots) + block, jnp.float32),
            pltpu.VMEM((rows, slots) + block, jnp.float32),
            pltpu.VMEM((GROUP, full, 2 * count), jnp.bfloat16),
            pltpu.VMEM((GROUP, LEVELS - 1) + block, jnp.float32),
            pltpu.SMEM((slots * 7,), jnp.int32),
            pltpu.SMEM((slots * 7,), jnp.float32),
            pltpu.SMEM((slots,), jnp.int32),
            dma((LEVELS,)),
            dma((RING,)),
            dma((2, LEVELS)),
            dma((LEVELS, plan.depth - 1)),
            dma((LEVELS, plan.depth - 1)),
            dma((groups, rows - 1)),
            dma((groups, rows - 1)),
            dma((groups, rows - 1)),
            dma((groups, rows - 1)),
        ],
        compiler_params=pltpu.CompilerParams(
            collective_id=0, has_side_effects=True, vmem_limit_bytes=60 * 1024 * 1024
        ),
    )(
        parent,
        pattern.reshape(slots * 7),
        node_sizes.reshape(slots),
        packed,
        inverse_rows.reshape(slots, piece, full),
        panels.reshape(slots, LEVELS - 1, piece, full),
    )
    return solved.reshape(slots, half, 2, count).swapaxes(1, 2).reshape(slots, 1, piece * count)


def solution(mesh):
    in_specs = (
        P(None, "pcol", "prow"),
        P(None, "pcol", "prow", None),
        P(None, "pcol", None, "prow", None),
        P(None, "pcol", None),
        P(None, "pcol"),
        P(),
    )
    out_specs = P(None, "pcol", "prow")
    return jax.shard_map(
        on_device, mesh=mesh, in_specs=in_specs, out_specs=out_specs, check_vma=False
    )
```

time: 917 us -> 246 us (0.27)
  waiting for transfers between devices: 623 us -> 0 us
  Pallas kernels: 0 us -> 225 us
  matrix products: 123 us -> 0 us
  local copies, waits for them, and re-layouts: 87.1 us -> 16.1 us
  other arithmetic: 51 us -> 4 us
  between operations: 24.6 us -> 0.04 us
    unnamed x21 -> x0, waiting for transfers between devices: 306 us -> none
    psum x8 -> x0, waiting for transfers between devices: 302 us -> none  [on_device(): summed = lax.psum(partial_term, 'prow')]
    pallas_call x0 -> x1, Pallas kernels: none -> 225 us  [on_device(): pl.pallas_call(functools.partial(kernel, plan), out_shape=jax.ShapeDtypeS...]
    dot_general x37 -> x0, matrix products: 123 us -> none  [the longest x7 62.4 us: on_device(): jnp.einsum('napw,nwq->napq', panel_rows, solved, precision=lax.Precision....]
    slice x49 -> x0, local copies, waits for them, and re-layouts: 32.8 us -> none  [the longest x33 28 us: on_device(): contrib[:, distance].reshape(level_slots, piece_len)]
    sub x29 -> x0, other arithmetic: 21.3 us -> none  [the longest x7 11.4 us: on_device(): residue = residue - collect_updates(pending[height], level_slots, col_count)]
    mul x17 -> x0, other arithmetic: 18.1 us -> none  [the longest x11 15.3 us: on_device(): summed.reshape(level_slots, full_rows, rhs_count) * keep_full[:, :, None]]
    gather x26 -> x0, local copies, waits for them, and re-layouts: 16.8 us -> none  [on_device(): ancestor = parent[ancestor]]
  transfers between devices with their start and end apart: 15 -> 0, of which waited for: 15 -> 0; matrix products, arithmetic and copies ran while one was open for 12% -> 0% of each run, Pallas kernels for 0% -> 0%
where the time goes in v1:
time: 246 us; the launch traced here: 245 us
  Pallas kernels  225 us (91%)
  local copies, waits for them, and re-layouts  16.1 us (7%)
  other arithmetic  4 us (2%)
    pallas_call x1, Pallas kernels, on_device(): pl.pallas_call(functools.partial(kernel, plan), out_shape=jax.ShapeDtypeS...  225 us
    reshape x3, local copies, waits for them, and re-layouts, on_device(): right_side.reshape(slots, 2, half, count).swapaxes(1, 2)  7.48 us
    reshape x2, local copies, waits for them, and re-layouts, on_device(): solved.reshape(slots, half, 2, count).swapaxes(1, 2)  6.11 us

profile of v1, /device:TPU:0, one launch (start us, length us, event | category | flops | bytes accessed | tf_op | source)
XLA Modules:
  0.0 245.4 jit_solution(13690291236637093002)
XLA Ops:
  0.0 4.0 %reduce = f32[34,8192]{1,0:T(8,128)S(1)} reduce(f32[34,1,8192]{2,1,0:T(1,128)} %param.6, f32[]{:T(128)} %constant.5), dimensions={1}, to_apply=%param.6.reduce_sub_computation | reduce | bytes 2228228 | tf_op args[0]
  4.0 0.9 reshape.26
  4.9 3.2 %copy.13 = f32[34,2,64,64]{3,1,2,0:T(2,128)} copy(f32[34,2,64,64]{3,2,1,0:T(8,128)S(1)} %reshape.26) | data formatting | bytes 2228224 | tf_op jit(solution)/shard_map/reshape | solution.py:324
  8.1 0.0 copy-start
  8.1 3.4 %reshape.27.rhs = f32[34,64,128]{2,1,0:T(8,128)} reshape(f32[34,64,2,64]{3,2,1,0:T(2,128)} %bitcast.13) | data formatting | bytes 2228224 | tf_op jit(solution)/shard_map/reshape | solution.py:324
  11.5 0.0 copy-done
  11.5 0.1 copy.9
  11.6 0.7 reshape.24.pattern
  12.3 225.3 %shard_map.64 = f32[34,64,128]{2,1,0:T(8,128)} custom-call(s32[254]{0:T(256)} %parent.1, s32[238]{0:T(256)} %reshape.24.pattern, s32[34]{0:T(128)} %bitcast.15, f32[34,64,128]{2,1,0:T(8,128)} %reshape.27.rhs, f32[34,128,512]{2,1,0:T(8,128)} %bitcast.12, f32[34,7,128,512]{3,2,1,0:T(8,128)} %bitcast.11), custom_call_target="tpu_custom_call" | custom-call | tf_op jit(solution)/shard_map/pallas_call | solution.py:331
  237.5 2.6 %reshape.30 = f32[34,64,2,64]{3,2,1,0:T(2,128)S(1)} reshape(f32[34,64,128]{2,1,0:T(8,128)} %shard_map.64) | data formatting | bytes 2228224 | tf_op jit(solution)/shard_map/reshape | solution.py:371
  240.1 1.7 copy.11
  241.8 3.5 %reshape.31 = f32[34,1,8192]{2,1,0:T(1,128)} reshape(f32[34,2,64,64]{3,2,1,0:T(8,128)} %copy.11) | data formatting | bytes 2228224 | tf_op jit(solution)/shard_map/reshape | solution.py:371
Async XLA Ops:
  8.1 3.4 %copy-start = (s32[34,1,7]{0,1,2:T(1,128)S(1)}, s32[34,1,7]{0,1,2:T(1,128)}, u32[]{:S(2)}) copy-start(s32[34,1,7]{0,1,2:T(1,128)} %param.9) | copy-start | bytes 2860

commit v2 on v1

--- a/solution.py
+++ b/solution.py
@@ -38,7 +38,8 @@
         self.total, self.pend, self.half, self.far = s, p, c, f
         self.groups = []
         for h in range(LEVELS):
-            size = min(GROUP, self.slots[h])
+            size = GROUP if h == 0 else min(2, max(1, self.slots[h] // 2))
+            size = min(size, self.slots[h])
             for start in range(0, self.slots[h], size):
                 self.groups.append((h, self.slot_base[h] + start, size))
         self.level_of = [h for h in range(LEVELS) for _ in range(self.slots[h])]
@@ -61,7 +62,7 @@
 def kernel(
     plan, parent, pattern, sizes, rhs, inverse_hbm, panels_hbm, out,
     inverse, ring, pend, near, far, parts, arrived, solved, wide, blocks,
-    target, weight, live,
+    target, weight, live, flip,
     inverse_sem, ring_sem, near_sem, far_send, far_recv, part_send, part_recv, sol_send, sol_recv,
 ):
     rows, cols, depth = plan.rows, plan.cols, plan.depth
@@ -109,7 +110,7 @@
             slot = plan.slot_base[h] + i
             place = i * cols + my_col
             real = place < plan.nodes[h]
-            live[slot] = jnp.where(real, sizes[slot], 0)
+            live[slot] = jnp.where(real, sizes[slot, 0], 0)
             node = plan.node_base[h] + jnp.minimum(place, plan.nodes[h] - 1)
             for a in range(LEVELS - 1 - h):
                 up = h + 1 + a
@@ -118,7 +119,7 @@
                 owner = lax.rem(local, cols)
                 spot = lax.rem(owner, 2) * depth + lax.div(owner, 2)
                 target[slot * 7 + a] = spot * plan.slots[up] + lax.div(local, cols)
-                weight[slot * 7 + a] = jnp.where(real, pattern[slot * 7 + a], 0).astype(jnp.float32)
+                weight[slot * 7 + a] = jnp.where(real, pattern[slot, 0, a], 0).astype(jnp.float32)
             return carry
 
         lax.fori_loop(0, plan.slots[h], describe, 0)
@@ -139,6 +140,15 @@
     contract_first = (((0,), (0,)), ((), ()))
     sends = []
 
+    def pack_halves(slot, carry):
+        pairs = rhs[slot]
+        flip[pl.ds(0, half, stride=2)] = pairs
+        flip[pl.ds(1, half, stride=2)] = pltpu.roll(pairs, 64, 1)
+        out[slot] = jnp.where(low_lanes, flip[:half], pltpu.roll(flip[half:], 64, 1))
+        return carry
+
+    lax.fori_loop(0, plan.total, pack_halves, 0)
+
     pl.semaphore_wait(barrier, len(greeted))
 
     def remote(src, dst, send_sem, recv_sem, who):
@@ -155,7 +165,7 @@
 
         def body(n, carry):
             slot = base + n
-            residue = rhs[slot]
+            residue = out[slot]
             if h > 0:
                 step = slot - plan.slot_base[h]
                 own = (my_core * depth + my_z) * plan.slots[h] + step
@@ -197,7 +207,10 @@
                 total = total + arrived[d, slot]
             total = jnp.where(row_ids < live[slot], total, 0.0)
             solved[my_row, slot] = total
-            out[slot] = total
+            flip[:half] = total
+            flip[half:] = pltpu.roll(total, 64, 1)
+            even, odd = flip[pl.ds(0, half, stride=2)], flip[pl.ds(1, half, stride=2)]
+            out[slot] = jnp.where(low_lanes, even, pltpu.roll(odd, 64, 1))
             return carry
 
         lax.fori_loop(0, size, body, 0)
@@ -270,47 +283,60 @@
         mine = plan.pend_base[h] + my_core * count
         copy.wait_recv()
 
-        def body(i, carry):
-            pend[mine + i] = pend[mine + i] + near[plan.half_base[h] + i]
-            return carry
-
-        lax.fori_loop(0, count, body, 0)
-        return [
-            remote(
-                pend.at[pl.ds(mine + z * plan.slots[h], plan.slots[h])],
-                far.at[pl.ds(plan.far_base[h] + d * plan.slots[h], plan.slots[h])],
-                far_send.at[h, d], far_recv.at[h, d], (my_row, z * 2 + my_core),
-            )
-            for d, z in enumerate(z_peers)
-        ]
+        for g in group_ids[h]:
+            _, base, size = plan.groups[g]
+            start = base - plan.slot_base[h]
+
+            def body(i, carry, start=start, size=size):
+                spot = lax.div(i, size) * plan.slots[h] + start + lax.rem(i, size)
+                pend[mine + spot] = pend[mine + spot] + near[plan.half_base[h] + spot]
+                return carry
+
+            lax.fori_loop(0, depth * size, body, 0)
+            arriving[g] = [
+                remote(
+                    pend.at[pl.ds(mine + z * plan.slots[h] + start, size)],
+                    far.at[pl.ds(plan.far_base[h] + d * plan.slots[h] + start, size)],
+                    far_send.at[g, d], far_recv.at[g, d], (my_row, z * 2 + my_core),
+                )
+                for d, z in enumerate(z_peers)
+            ]
 
     group_ids = {h: [g for g, one in enumerate(plan.groups) if one[0] == h] for h in range(LEVELS)}
+    arriving = {}
+
+    def finish(g):
+        h, base, size = plan.groups[g]
+        reach = LEVELS - 1 - h
+        if reach == 0:
+            return
+        final = g == group_ids[h][-1]
+        widen(g, sharing[g])
+        contribute(g, 0, 1)
+        if final:
+            near_copy = start_near(h + 1)
+        contribute(g, 1, min(2, reach))
+        if final:
+            start_far(h + 1, near_copy)
+        contribute(g, 2, reach)
+        for slot in range(base, base + size):
+            load_panel(slot + RING)
+
+    waiting, sharing = {}, {}
     for h in range(LEVELS):
-        reach = LEVELS - 1 - h
         ids = group_ids[h]
         loads[h].wait()
-        waiting = [start_partial(g) for g in ids]
-        sharing = {ids[0]: start_solved(ids[0], waiting[0])}
-        for i, g in enumerate(ids):
-            if i + 1 < len(ids):
-                sharing[ids[i + 1]] = start_solved(ids[i + 1], waiting[i + 1])
-            if reach == 0:
-                continue
-            widen(g, sharing[g])
-            final = i + 1 == len(ids)
-            contribute(g, 0, 1)
-            if final:
-                near_copy = start_near(h + 1)
-            contribute(g, 1, min(2, reach))
-            if final:
-                far_copies = start_far(h + 1, near_copy)
-            contribute(g, 2, reach)
-            _, base, size = plan.groups[g]
-            for slot in range(base, base + size):
-                load_panel(slot + RING)
-            if final:
-                for copy in far_copies:
+        if h == 0:
+            waiting.update({g: start_partial(g) for g in ids})
+        for i in range(len(ids) + 2):
+            if i < len(ids) and h > 0:
+                for copy in arriving[ids[i]]:
                     copy.wait_recv()
+                waiting[ids[i]] = start_partial(ids[i])
+            if 0 <= i - 1 < len(ids):
+                sharing[ids[i - 1]] = start_solved(ids[i - 1], waiting[ids[i - 1]])
+            if i >= 2:
+                finish(ids[i - 2])
     for copy in sends:
         copy.wait_send()
 
@@ -321,7 +347,7 @@
     slots, piece, full = plan.total, panels.shape[3], panels.shape[4]
     count = right_side.shape[2] // piece
     half = piece // 2
-    packed = right_side.reshape(slots, 2, half, count).swapaxes(1, 2).reshape(slots, half, 2 * count)
+    packed = right_side.reshape(slots, half, 2 * count)
     groups = len(plan.groups)
     dma = pltpu.SemaphoreType.DMA
     vmem = pl.BlockSpec(memory_space=pltpu.VMEM)
@@ -347,11 +373,12 @@
             pltpu.SMEM((slots * 7,), jnp.int32),
             pltpu.SMEM((slots * 7,), jnp.float32),
             pltpu.SMEM((slots,), jnp.int32),
+            pltpu.VMEM((piece, 2 * count), jnp.float32),
             dma((LEVELS,)),
             dma((RING,)),
             dma((2, LEVELS)),
-            dma((LEVELS, plan.depth - 1)),
-            dma((LEVELS, plan.depth - 1)),
+            dma((groups, plan.depth - 1)),
+            dma((groups, plan.depth - 1)),
             dma((groups, rows - 1)),
             dma((groups, rows - 1)),
             dma((groups, rows - 1)),
@@ -362,13 +389,13 @@
         ),
     )(
         parent,
-        pattern.reshape(slots * 7),
-        node_sizes.reshape(slots),
+        pattern,
+        node_sizes,
         packed,
         inverse_rows.reshape(slots, piece, full),
         panels.reshape(slots, LEVELS - 1, piece, full),
     )
-    return solved.reshape(slots, half, 2, count).swapaxes(1, 2).reshape(slots, 1, piece * count)
+    return solved.reshape(slots, 1, piece * count)
 
 
 def solution(mesh):

time: 246 us -> 218 us (0.89)
  Pallas kernels: 225 us -> 212 us
  local copies, waits for them, and re-layouts: 16.1 us -> 5.09 us
  other arithmetic: 4 us -> 0 us
    reshape x6 -> x0, local copies, waits for them, and re-layouts: 14.3 us -> none  [the longest x3 7.48 us: on_device(): right_side.reshape(slots, 2, half, count).swapaxes(1, 2)]
    pallas_call x1, Pallas kernels: 225 us -> 212 us  [on_device(): pl.pallas_call(functools.partial(kernel, plan), out_shape=jax.ShapeDtypeS...]
    unnamed x3, local copies, waits for them, and re-layouts: 0.1 us -> 5.09 us
    unnamed x1 -> x0, other arithmetic: 4 us -> none
where the time goes in v2:
time: 218 us; the launch traced here: 217 us
  Pallas kernels  212 us (97%)
  local copies, waits for them, and re-layouts  5.09 us (2%)
    pallas_call x1, Pallas kernels, on_device(): pl.pallas_call(functools.partial(kernel, plan), out_shape=jax.ShapeDtypeS...  212 us
    unnamed x3, local copies, waits for them, and re-layouts  5.09 us

profile of v2, /device:TPU:0, one launch (start us, length us, event | category | flops | bytes accessed | tf_op | source)
XLA Modules:
  0.0 217.5 jit_solution(14870025507611346673)
XLA Ops:
  0.0 1.4 copy.10.pattern
  1.4 1.3 copy.11.sizes
  2.7 212.4 %shard_map.64 = f32[34,64,128]{2,1,0:T(8,128)} custom-call(s32[254]{0:T(256)} %parent.1, s32[34,1,7]{2,1,0:T(1,128)} %copy.10.pattern, s32[34,1]{1,0:T(8,128)} %copy.11.sizes, f32[34,64,128]{2,1,0:T(8,128)} %bitcast.7, f32[34,128,512]{2,1,0:T(8,128)} %bitcast.5, f32[34,7,128,512]{3,2,1,0:T(8,128)} %bitcast.4), custom_call_target="tpu_custom_call" | custom-call | tf_op jit(solution)/shard_map/pallas_call | solution.py:357
  215.1 2.4 %copy.14 = f32[34,1,8192]{2,1,0:T(1,128)} copy(f32[34,1,8192]{2,1,0:T(1,128)} %bitcast.6) | data formatting | bytes 2228224

commit v3 on v2

--- a/solution.py
+++ b/solution.py
@@ -11,6 +11,7 @@
 LEAVES = 128
 GROUP = 4
 RING = 12
+WIDE = 16
 MESH = pl.DeviceIdType.MESH
 
 
@@ -106,29 +107,39 @@
 
     for h in range(LEVELS):
 
-        def describe(i, carry, h=h):
+        def measure_live(i, carry, h=h):
             slot = plan.slot_base[h] + i
-            place = i * cols + my_col
-            real = place < plan.nodes[h]
-            live[slot] = jnp.where(real, sizes[slot, 0], 0)
-            node = plan.node_base[h] + jnp.minimum(place, plan.nodes[h] - 1)
-            for a in range(LEVELS - 1 - h):
-                up = h + 1 + a
-                node = parent[node]
-                local = node - plan.node_base[up]
-                owner = lax.rem(local, cols)
-                spot = lax.rem(owner, 2) * depth + lax.div(owner, 2)
-                target[slot * 7 + a] = spot * plan.slots[up] + lax.div(local, cols)
-                weight[slot * 7 + a] = jnp.where(real, pattern[slot, 0, a], 0).astype(jnp.float32)
-            return carry
-
-        lax.fori_loop(0, plan.slots[h], describe, 0)
-
-    def clear(i, carry):
-        pend[i] = jnp.zeros_like(pend[i])
-        return carry
-
-    lax.fori_loop(0, plan.pend, clear, 0)
+            live[slot] = jnp.where(i * cols + my_col < plan.nodes[h], sizes[slot, 0], 0)
+            return carry
+
+        lax.fori_loop(0, plan.slots[h], measure_live, 0)
+
+    def describe_targets():
+        for h in range(LEVELS):
+
+            def describe(i, carry, h=h):
+                slot = plan.slot_base[h] + i
+                place = i * cols + my_col
+                real = place < plan.nodes[h]
+                node = plan.node_base[h] + jnp.minimum(place, plan.nodes[h] - 1)
+                for a in range(LEVELS - 1 - h):
+                    up = h + 1 + a
+                    node = parent[node]
+                    local = node - plan.node_base[up]
+                    owner = lax.rem(local, cols)
+                    spot = lax.rem(owner, 2) * depth + lax.div(owner, 2)
+                    target[slot * 7 + a] = spot * plan.slots[up] + lax.div(local, cols)
+                    weight[slot * 7 + a] = jnp.where(real, pattern[slot, 0, a], 0).astype(jnp.float32)
+                return carry
+
+            lax.fori_loop(0, plan.slots[h], describe, 0)
+
+        def clear(i, carry):
+            pend[i] = jnp.zeros_like(pend[i])
+            return carry
+
+        lax.fori_loop(0, plan.pend, clear, 0)
+        lax.fori_loop(plan.slots[0], plan.total, pack_halves, 0)
 
     lane = lax.broadcasted_iota(jnp.int32, (half, 128), 1)
     low_lanes = lane < 64
@@ -147,7 +158,7 @@
         out[slot] = jnp.where(low_lanes, flip[:half], pltpu.roll(flip[half:], 64, 1))
         return carry
 
-    lax.fori_loop(0, plan.total, pack_halves, 0)
+    lax.fori_loop(0, plan.slots[0], pack_halves, 0)
 
     pl.semaphore_wait(barrier, len(greeted))
 
@@ -232,7 +243,7 @@
 
         def body(n, carry):
             for r in range(rows):
-                wide[n, pl.ds(r * piece, piece)] = split_pair(solved[r, base + n], low_lanes)
+                wide[lax.rem(base + n, WIDE), pl.ds(r * piece, piece)] = split_pair(solved[r, base + n], low_lanes)
             return carry
 
         lax.fori_loop(0, size, body, 0)
@@ -246,7 +257,7 @@
 
         def body(n, carry):
             place = lax.rem(base + n, RING)
-            pair = wide[n]
+            pair = wide[lax.rem(base + n, WIDE)]
             for a in range(first, last):
                 high, low = two_part(ring[place, a])
                 both = jnp.dot(high, pair, preferred_element_type=jnp.float32)
@@ -315,19 +326,37 @@
         contribute(g, 0, 1)
         if final:
             near_copy = start_near(h + 1)
-        contribute(g, 1, min(2, reach))
+        if final or h > 0 or g == 0:
+            contribute(g, 1, min(2, reach))
         if final:
             start_far(h + 1, near_copy)
-        contribute(g, 2, reach)
+        if h == 0 and g > 0:
+            later.append((g, 2 if final else 1))
+        else:
+            contribute(g, 2, reach)
+            release(g)
+
+    def release(g):
+        _, base, size = plan.groups[g]
         for slot in range(base, base + size):
             load_panel(slot + RING)
 
+    def catch_up():
+        if later:
+            g, first = later.pop(0)
+            contribute(g, first, LEVELS - 1)
+            release(g)
+
+    later = []
     waiting, sharing = {}, {}
     for h in range(LEVELS):
         ids = group_ids[h]
         loads[h].wait()
         if h == 0:
             waiting.update({g: start_partial(g) for g in ids})
+            describe_targets()
+        if h == 1:
+            catch_up()
         for i in range(len(ids) + 2):
             if i < len(ids) and h > 0:
                 for copy in arriving[ids[i]]:
@@ -335,7 +364,11 @@
                 waiting[ids[i]] = start_partial(ids[i])
             if 0 <= i - 1 < len(ids):
                 sharing[ids[i - 1]] = start_solved(ids[i - 1], waiting[ids[i - 1]])
+            if h > 0:
+                catch_up()
             if i >= 2:
+                while later and h > 0:
+                    catch_up()
                 finish(ids[i - 2])
     for copy in sends:
         copy.wait_send()
@@ -368,7 +401,7 @@
             pltpu.VMEM((rows, slots) + block, jnp.float32),
             pltpu.VMEM((rows - 1, slots) + block, jnp.float32),
             pltpu.VMEM((rows, slots) + block, jnp.float32),
-            pltpu.VMEM((GROUP, full, 2 * count), jnp.bfloat16),
+            pltpu.VMEM((WIDE, full, 2 * count), jnp.bfloat16),
             pltpu.VMEM((GROUP, LEVELS - 1) + block, jnp.float32),
             pltpu.SMEM((slots * 7,), jnp.int32),
             pltpu.SMEM((slots * 7,), jnp.float32),

time: 218 us -> 211 us (0.968)
  Pallas kernels: 212 us -> 206 us
    pallas_call x1, Pallas kernels: 212 us -> 206 us  [on_device(): pl.pallas_call(functools.partial(kernel, plan), out_shape=jax.ShapeDtypeS...]
where the time goes in v3:
time: 211 us
  Pallas kernels  206 us (98%)
  local copies, waits for them, and re-layouts  5.09 us (2%)
    pallas_call x1, Pallas kernels, on_device(): pl.pallas_call(functools.partial(kernel, plan), out_shape=jax.ShapeDtypeS...  206 us
    unnamed x3, local copies, waits for them, and re-layouts  5.09 us

profile of v3, /device:TPU:0, one launch (start us, length us, event | category | flops | bytes accessed | tf_op | source)
XLA Modules:
  0.0 210.8 jit_solution(15389050119025916533)
XLA Ops:
  0.0 1.4 copy.10.pattern
  1.4 1.3 copy.11.sizes
  2.7 205.7 %shard_map.64 = f32[34,64,128]{2,1,0:T(8,128)} custom-call(s32[254]{0:T(256)} %parent.1, s32[34,1,7]{2,1,0:T(1,128)} %copy.10.pattern, s32[34,1]{1,0:T(8,128)} %copy.11.sizes, f32[34,64,128]{2,1,0:T(8,128)} %bitcast.7, f32[34,128,512]{2,1,0:T(8,128)} %bitcast.5, f32[34,7,128,512]{3,2,1,0:T(8,128)} %bitcast.4), custom_call_target="tpu_custom_call" | custom-call | tf_op jit(solution)/shard_map/pallas_call | solution.py:390
  208.5 2.4 %copy.14 = f32[34,1,8192]{2,1,0:T(1,128)} copy(f32[34,1,8192]{2,1,0:T(1,128)} %bitcast.6) | data formatting | bytes 2228224
